TPU v7x, 256 devices: a whole 4x4x8 slice. The times are simulated.
256 devices in a mesh: outer: 16 (over z, y_hi), inner: 16 (over y_lo, x, core).
Axes of the slice: x: 4, y: 4 (y_hi: 2, y_lo: 2; y = y_hi * 2 + y_lo), z: 8, core: 2. Of those that a mesh axis runs over, the one named last changes fastest.
Arguments:
- queries: bfloat16 [32768, 32, 128], P(('outer', 'inner')), may hold values from -6 to 6
- keys: bfloat16 [32768, 4, 128], P(('outer', 'inner')), may hold values from -6 to 6
- values: bfloat16 [32768, 4, 128], P(('outer', 'inner')), may hold values from -6 to 6
- output_gradient: bfloat16 [32768, 32, 128], P(('outer', 'inner')), may hold values from -6 to 6
- kept_offset: int32 [256, 128], replicated, may hold values from 0 to 1024, as said below
- region_pos: int32 [256], replicated, may hold values from 0 to 255, each once
Outputs:
- attn_out: bfloat16 [32768, 32, 128], P(('outer', 'inner'))
- grad_queries: bfloat16 [32768, 32, 128], P(('outer', 'inner'))
- key_gradient: bfloat16 [32768, 4, 128], P(('outer', 'inner'))
- value_gradient: bfloat16 [32768, 4, 128], P(('outer', 'inner'))
Inputs may be any that keep to these rules, and one draw needn't show every extreme that they name: In each row of kept_offset the live slots (values under 1024) come first and strictly increase; the remaining slots hold 1024. Every shard has at least two live slots, some shard has all 128 live with offset 0 in its first slot, and some shard has empty slots.
All inputs are finite; a program needn't handle non-finite values.
Results may differ from a plain program's by a relative error of at most 0.025.
Values may be sent and summed in bfloat16 or wider, within the bound.
No kernel may reach another device: no remote copies, remote signals or barrier semaphores. Data moves between devices by JAX's collectives and lax.ppermute only.
A program may use at most 128 MiB of HBM per device.

v0:
```python
import functools
import math

import jax
import jax.numpy as jnp
from jax import lax
from jax.experimental import pallas as pl
from jax.experimental.pallas import tpu as pltpu
from jax.sharding import Mesh
from jax.sharding import PartitionSpec as P

REGION = 1024
SLOTS = 128
WIDTH = 128
HEADS_Q = 32
HEADS_KV = 4
N_OUTER = 16
N_Y = 2
N_X = 4
N_CORE = 2
WINDOW = 32
KEY_ROWS = WINDOW * SLOTS
PIECES = 8

QUERY_AXES = ("x", "core")
SHARDS = N_X * N_CORE
HEADS = HEADS_Q // SHARDS
QUERY_ROWS = SHARDS * SLOTS
TILES = SHARDS
LANES = HEADS * SLOTS
UNIT = 256
SPAN = 512
UNITS = KEY_ROWS // UNIT
SAFE = 60.0

FILL = -1e30
FLOOR = -1e29
SCALE = WIDTH ** (-0.5)
BASE_TWO = SCALE * math.log2(math.e)
BF16, F32, I32 = jnp.bfloat16, jnp.float32, jnp.int32

KEY_ORDER = 0
KEY_OFFSET = 32
KEY_COUNT = 64
QUERY_ORDER = 96
QUERY_OFFSET = 112
QUERY_COUNT = 128
QUERY_KEY = 144
REACH = 160
TILE_COUNT = 176


def slots():
    return lax.broadcasted_iota(I32, (SLOTS, WIDTH), 0)


def up(n, unit):
    return (n + unit - 1) // unit


def tile_rows(i):
    return pl.ds(pl.multiple_of(i * SLOTS, SLOTS), SLOTS)


def unit_rows(u, rows):
    return pl.ds(pl.multiple_of(u * UNIT, UNIT), rows)


def pack_rows(sc, array, part, packed):
    slot = slots()
    packed[:, tile_rows(sc[TILE_COUNT] - 1), :] = jnp.zeros((HEADS, SLOTS, WIDTH), F32)

    @pl.loop(0, SHARDS)
    def _(j):
        s = sc[QUERY_ORDER + j]
        live = (slot < sc[QUERY_COUNT + s])[None]
        packed[:, pl.ds(sc[QUERY_OFFSET + s], SLOTS), :] = jnp.where(
            live, array[s, part].astype(F32), 0.0
        )


def unpack_rows(sc, packed, array, part):
    slot = slots()

    @pl.loop(0, SHARDS)
    def _(s):
        live = (slot < sc[QUERY_COUNT + s])[None]
        rows = packed[:, pl.ds(sc[QUERY_OFFSET + s], SLOTS), :]
        array[s, part] = jnp.where(live, rows, 0.0).astype(BF16)


def shown(s, first, limit):
    place = lax.broadcasted_iota(I32, s.shape, 0)
    return jnp.where(place <= limit - first, s, FILL)


def fold(op, s):
    return op(s.reshape(-1, 8, s.shape[1]), axis=0)


def square(a):
    a = a.astype(F32)
    return jnp.sum(a * a, axis=0, keepdims=True)


def prepare(sc, *refs):
    pieces, (kc, vc, kt, vt, long_ref, stage, kf, vf, sems) = refs[:PIECES], refs[PIECES:]
    spans = up(sc[REACH + sc[TILE_COUNT] - 1], SPAN)
    copies = [
        pltpu.make_async_copy(ref, stage.at[pl.ds(p * N_X, N_X)], sems.at[p])
        for p, ref in enumerate(pieces)
    ]
    for copy in copies:
        copy.start()
    tail = pl.ds(pl.multiple_of((spans - 1) * SPAN, SPAN), SPAN)
    kf[tail, :] = jnp.zeros((SPAN, WIDTH), F32)
    vf[tail, :] = jnp.zeros((SPAN, WIDTH), F32)
    for copy in copies:
        copy.wait()

    @pl.loop(0, WINDOW)
    def _(j):
        w = sc[KEY_ORDER + j]
        rows = pl.ds(sc[KEY_OFFSET + w], SLOTS)
        kf[rows, :] = stage[w, 0].astype(F32)
        vf[rows, :] = stage[w, 1].astype(F32)

    def turn(n, longest):
        rows = pl.ds(pl.multiple_of(n * SPAN, SPAN), SPAN)
        keys = kf[rows, :].astype(BF16)
        vals = vf[rows, :].astype(BF16)
        kc[rows, :] = keys
        vc[rows, :] = vals
        keys = keys.T
        kt[n] = keys
        vt[n] = vals.T
        return jnp.maximum(longest, square(keys))

    long_ref[...] = lax.fori_loop(0, spans, turn, jnp.zeros((1, SPAN), F32))


def attend(sc, long_ref, rows_ref, *refs):
    keys_refs, (out_ref, *term_refs), scratch = refs[:4], refs[4:7], refs[7:]
    raw, kc, vc, kt, vt, qf, gf, thr, limits, qt, gt, ot, dqt = scratch[:13]
    wb, wn, db, dk, dv, terms, sems, out_sems = scratch[13:]
    slot = slots()
    tiles = sc[TILE_COUNT]

    copies = [
        pltpu.make_async_copy(ref, place, sems.at[n])
        for n, (ref, place) in enumerate(zip((rows_ref, *keys_refs), (raw, kc, vc, kt, vt)))
    ]
    for copy in copies:
        copy.start()

    thr[tile_rows(tiles - 1), :] = jnp.full((SLOTS, WIDTH), -1, I32)

    @pl.loop(0, UNITS)
    def _(u):
        dk[unit_rows(u, UNIT), :] = jnp.zeros((UNIT, WIDTH), F32)
        dv[unit_rows(u, UNIT), :] = jnp.zeros((UNIT, WIDTH), F32)

    @pl.loop(0, SHARDS)
    def _(j):
        s = sc[QUERY_ORDER + j]
        thr[pl.ds(sc[QUERY_OFFSET + s], SLOTS), :] = jnp.where(
            slot < sc[QUERY_COUNT + s], slot + sc[QUERY_KEY + s], -1
        )

    longest = jnp.max(long_ref[...])
    copies[0].wait()
    pack_rows(sc, raw, 0, qf)
    pack_rows(sc, raw, 1, gf)
    for copy in copies[1:]:
        copy.wait()

    def turn(i, longest_row):
        rows = tile_rows(i)
        limits[i] = jnp.concatenate([thr[rows, :].T[0:1, :]] * HEADS, axis=1)
        q_turn = qf[:, rows, :].astype(BF16).reshape(LANES, WIDTH).T
        qt[i] = q_turn
        gt[i] = gf[:, rows, :].astype(BF16).reshape(LANES, WIDTH).T
        return jnp.maximum(longest_row, square(q_turn))

    longest_row = jnp.max(lax.fori_loop(0, tiles, turn, jnp.zeros((1, LANES), F32)))
    safe = longest_row * longest * BASE_TWO ** 2 <= SAFE ** 2

    @pl.loop(0, tiles)
    def _(i):
        rows = tile_rows(i)
        count = up(sc[REACH + i], SPAN)
        limit = limits[i]
        q_turn = qt[i]

        def span_rows(n):
            return pl.ds(pl.multiple_of(n * SPAN, SPAN), SPAN)

        def scores(n):
            s = jnp.dot(kc[span_rows(n), :], q_turn, preferred_element_type=F32)
            return shown(s, n * SPAN, limit)

        top = lax.fori_loop(
            0,
            jnp.where(safe, 0, count),
            lambda n, top: jnp.maximum(top, fold(jnp.max, scores(n))),
            jnp.full((8, LANES), jnp.where(safe, 0.0, FLOOR), F32),
        )
        top = jnp.max(top, axis=0, keepdims=True) * BASE_TWO

        def weigh(n):
            w = jnp.exp2(scores(n) * BASE_TWO - top)
            low = w.astype(BF16)
            wb[span_rows(n), :] = low
            wn[...] = low
            return fold(jnp.sum, w)

        def mix(n):
            return jnp.dot(vt[n], wn[...], preferred_element_type=F32)

        def step(n, carry):
            total, acc = carry
            acc = acc + mix(n - 1)
            return total + weigh(n), acc

        total = weigh(0)
        total, acc = lax.fori_loop(1, count, step, (total, jnp.zeros((WIDTH, LANES), F32)))
        acc = acc + mix(count - 1)
        total = jnp.sum(total, axis=0, keepdims=True)
        inverse = 1.0 / jnp.where(total > 0.0, total, 1.0)
        out = (acc * inverse).astype(BF16)
        ot[i] = out

        g_turn = gt[i]
        delta = jnp.sum(g_turn.astype(F32) * out.astype(F32), axis=0, keepdims=True)
        by_row = jnp.stack([
            jnp.broadcast_to(inverse[:, h * SLOTS : (h + 1) * SLOTS], (SLOTS, SLOTS)).T
            for h in range(HEADS)
        ])
        q_tile = (qf[:, rows, :] * by_row).astype(BF16).reshape(LANES, WIDTH)
        g_tile = (gf[:, rows, :] * by_row).astype(BF16).reshape(LANES, WIDTH)

        def weigh_back(n):
            at = span_rows(n)
            dp = jnp.dot(vc[at, :], g_turn, preferred_element_type=F32)
            db[...] = (wb[at, :].astype(F32) * (dp - delta)).astype(BF16)

        def mix_back(n, acc):
            at = span_rows(n)
            dv[at, :] += jnp.dot(wb[at, :], g_tile, preferred_element_type=F32)
            dk[at, :] += jnp.dot(db[...], q_tile, preferred_element_type=F32)
            return acc + jnp.dot(kt[n], db[...], preferred_element_type=F32)

        def step_back(n, acc):
            acc = mix_back(n - 1, acc)
            weigh_back(n)
            return acc

        weigh_back(0)
        acc = lax.fori_loop(1, count, step_back, jnp.zeros((WIDTH, LANES), F32))
        acc = mix_back(count - 1, acc)
        dqt[i] = (acc * (inverse * SCALE)).astype(BF16)

    out_copies = [
        pltpu.make_async_copy(terms.at[far], term_refs[far], out_sems.at[far]) for far in range(2)
    ]
    out_copies += [
        pltpu.make_async_copy(raw.at[:, part], out_ref.at[:, part], out_sems.at[2 + part])
        for part in range(2)
    ]
    for far in range(2):
        for g in range(2):

            @pl.loop(0, 2 * N_X)
            def _(e, g=g, far=far):
                y, x = e // N_X, e % N_X
                w = g * 16 + far * 8 + e
                rows = pl.ds(sc[KEY_OFFSET + w], SLOTS)
                live = slot < sc[KEY_COUNT + w]
                terms[far, g, y, x, 0] = jnp.where(live, dk[rows, :] * SCALE, 0.0).astype(BF16)
                terms[far, g, y, x, 1] = jnp.where(live, dv[rows, :], 0.0).astype(BF16)

        out_copies[far].start()

    for part, (turned, packed) in enumerate(((ot, qf), (dqt, gf))):

        @pl.loop(0, tiles)
        def _(i, turned=turned, packed=packed):
            rows = turned[i].T.astype(F32).reshape(HEADS, SLOTS, WIDTH)
            packed[:, tile_rows(i), :] = rows

        unpack_rows(sc, packed, raw, part)
        out_copies[2 + part].start()

    for copy in out_copies:
        copy.wait()


ROWS = (SHARDS, 2, HEADS, SLOTS, WIDTH)
KEYS = (KEY_ROWS, WIDTH)
TURNED_KEYS = (KEY_ROWS // SPAN, WIDTH, SPAN)
PACKING_KEYS = pltpu.VMEM((KEY_ROWS + SLOTS, WIDTH), F32)
PACKING_ROWS = pltpu.VMEM((HEADS, QUERY_ROWS + SLOTS, WIDTH), F32)


def call(kernel, operands, spaces, out_shape, out_space, scratch, flops, limit, name):
    return pl.pallas_call(
        kernel,
        out_shape=out_shape,
        in_specs=[pl.BlockSpec(memory_space=space) for space in spaces],
        out_specs=(pl.BlockSpec(memory_space=out_space),) * len(out_shape),
        scratch_shapes=scratch,
        compiler_params=pltpu.CompilerParams(vmem_limit_bytes=limit << 20),
        cost_estimate=pl.CostEstimate(flops=flops, bytes_accessed=6 << 20, transcendentals=0),
        name=name,
    )(*operands)


def prepare_keys(scalars, pieces):
    shape = jax.ShapeDtypeStruct
    return call(
        prepare,
        (scalars, *pieces),
        (pltpu.SMEM,) + (pltpu.HBM,) * PIECES,
        (
            shape(KEYS, BF16),
            shape(KEYS, BF16),
            shape(TURNED_KEYS, BF16),
            shape(TURNED_KEYS, BF16),
            shape((1, SPAN), F32),
        ),
        pltpu.VMEM,
        [
            pltpu.VMEM((WINDOW, 2, SLOTS, WIDTH), BF16),
            PACKING_KEYS,
            PACKING_KEYS,
            pltpu.SemaphoreType.DMA((PIECES,)),
        ],
        1 << 20,
        56,
        "window_keys",
    )


def attention(scalars, rows, packed):
    *keys, longest = packed
    terms = jax.ShapeDtypeStruct((2, 2, N_X, 2, SLOTS, WIDTH), BF16)
    return call(
        attend,
        (scalars, longest, rows, *keys),
        (pltpu.SMEM, pltpu.VMEM, pl.ANY) + (pltpu.HBM,) * 4,
        (jax.ShapeDtypeStruct(ROWS, BF16), terms, terms),
        pltpu.HBM,
        [
            pltpu.VMEM(ROWS, BF16),
            *[pltpu.VMEM(KEYS, BF16)] * 2,
            *[pltpu.VMEM(TURNED_KEYS, BF16)] * 2,
            *[PACKING_ROWS] * 2,
            pltpu.VMEM((QUERY_ROWS + SLOTS, WIDTH), I32),
            pltpu.VMEM((TILES, 1, LANES), I32),
            *[pltpu.VMEM((TILES, WIDTH, LANES), BF16)] * 4,
            pltpu.VMEM((KEY_ROWS, LANES), BF16),
            pltpu.VMEM((SPAN, LANES), BF16),
            pltpu.VMEM((SPAN, LANES), BF16),
            *[PACKING_KEYS] * 2,
            pltpu.VMEM((2, *terms.shape), BF16),
            pltpu.SemaphoreType.DMA((5,)),
            pltpu.SemaphoreType.DMA((4,)),
        ],
        20 << 30,
        42,
        "window_attention",
    )


def plan(kept_offset, region_pos):
    outer, y, x_, core = (lax.axis_index(a) for a in ("outer", "y", "x", "core"))
    shard = jnp.arange(N_OUTER * N_Y * N_X * N_CORE)
    counts = jnp.sum((kept_offset < REGION).astype(jnp.int32), axis=1)

    def pick(ids):
        hit = ids[:, None] == shard[None, :]
        of = lambda a: jnp.sum(jnp.where(hit, a[None, :], 0), axis=1)
        return of(counts), of(region_pos)

    w = jnp.arange(WINDOW)
    g, p, x = w // 16, w // 4 % 4, (x_ - w) % 4
    group = jnp.where(g == 0, outer, (outer - 1) % N_OUTER)
    count, place = pick(
        group * 16 + ((y ^ (p % 2)) * N_X + x) * N_CORE + (core ^ (p // 2))
    )
    before = place[None, :] < place[:, None]
    offset = jnp.sum(jnp.where(before, count[None, :], 0), axis=1)
    rank = jnp.sum(before.astype(jnp.int32), axis=1)
    order = jnp.sum(jnp.where(rank[None, :] == w[:, None], w[None, :], 0), axis=1)

    s = jnp.arange(SHARDS)
    q_count, q_place = pick(outer * 16 + (y * N_X + s // 2) * N_CORE + s % 2)
    q_before = q_place[None, :] < q_place[:, None]
    q_offset = jnp.sum(jnp.where(q_before, q_count[None, :], 0), axis=1)
    q_rank = jnp.sum(q_before.astype(jnp.int32), axis=1)
    q_order = jnp.sum(jnp.where(q_rank[None, :] == s[:, None], s[None, :], 0), axis=1)
    q_key = jnp.sum(jnp.where(place[None, :] < q_place[:, None], count[None, :], 0), axis=1)

    start = jnp.arange(TILES)[:, None] * SLOTS
    within = (q_offset[None, :] < start + SLOTS) & (q_offset[None, :] + q_count[None, :] > start)
    end = q_key[None, :] + jnp.minimum(q_count[None, :], start + SLOTS - q_offset[None, :])
    reach = jnp.max(jnp.where(within, end, 0), axis=1)
    tiles = (jnp.sum(q_count) + SLOTS - 1) // SLOTS

    pad = lambda a, n: jnp.pad(a, (0, n - a.shape[0]))
    return jnp.concatenate([
        order, offset, count,
        pad(q_order, 16), pad(q_offset, 16), pad(q_count, 16), pad(q_key, 16), pad(reach, 16),
        tiles[None],
    ]).astype(jnp.int32)


def total(*parts):
    return functools.reduce(jnp.add, [a.astype(F32) for a in parts]).astype(BF16)


def to_x(block, step):
    return lax.ppermute(block, "x", [(i, (i + step) % N_X) for i in range(N_X)])


def to_core(block):
    return lax.ppermute(block, "core", [(0, 1), (1, 0)])


def to_group(block, step, flip):
    route = [
        (i * 2 + y, (i + step) % N_OUTER * 2 + (y ^ flip))
        for i in range(N_OUTER)
        for y in range(N_Y)
    ]
    return lax.ppermute(block, ("outer", "y"), route)


def on_device(queries, keys, values, output_gradient, kept_offset, region_pos):
    x = lax.axis_index("x")
    exchange = functools.partial(lax.all_to_all, split_axis=0, concat_axis=0, tiled=True)
    kv = jnp.stack([keys, values]).transpose(2, 0, 1, 3)
    kv = [lax.dynamic_index_in_dim(kv, (x + k) % N_X, 0, keepdims=False) for k in range(N_X)]
    own = jnp.stack([to_x(kv[k], k) if k else kv[0] for k in range(N_X)])

    def by_head(a):
        return a.transpose(1, 0, 2).reshape(SHARDS, HEADS, SLOTS, WIDTH)

    rows = jnp.stack([by_head(queries), by_head(output_gradient)], axis=1)
    own, rows, kept_offset, region_pos = lax.optimization_barrier(
        (own, rows, kept_offset, region_pos)
    )
    scalars = plan(kept_offset, region_pos)
    own_pair = (own, to_group(own, 0, 1))
    prev_pair = (to_group(own, 1, 0), to_group(own, 1, 1))
    pieces = (
        *own_pair, *(to_core(a) for a in own_pair), *prev_pair, *(to_core(a) for a in prev_pair)
    )

    rows = exchange(rows, QUERY_AXES)
    rows, near, far = attention(scalars, rows, prepare_keys(scalars, pieces))
    far = to_core(far)
    term = lambda g, y: total(near[g, y], far[g, y])
    sums = total(
        term(0, 0),
        to_group(term(0, 1), 0, 1),
        to_group(term(1, 0), -1, 0),
        to_group(term(1, 1), -1, 1),
    )
    grads = [to_x(sums[k], -k) if k else sums[0] for k in range(N_X)]
    grads = jnp.stack([lax.select_n((h - x) % N_X, *grads) for h in range(N_X)])
    home = exchange(rows, QUERY_AXES)

    def by_slot(a):
        return a.reshape(HEADS_Q, SLOTS, WIDTH).transpose(1, 0, 2)

    return (
        by_slot(home[:, 0]),
        by_slot(home[:, 1]),
        grads[:, 0].transpose(1, 0, 2),
        grads[:, 1].transpose(1, 0, 2),
    )


def solution(mesh):
    devices = mesh.devices.reshape(N_OUTER, N_Y, N_X, N_CORE)
    split = Mesh(devices, ("outer", "y", "x", "core"))
    rows = P(("outer", "y", "x", "core"), None, None)
    return jax.shard_map(
        on_device,
        mesh=split,
        in_specs=(rows, rows, rows, rows, P(), P()),
        out_specs=(rows, rows, rows, rows),
        check_vma=False,
    )
```

profile of v0, /device:TPU:2, one launch (start us, length us, event | category | flops | bytes accessed | tf_op | source)
XLA Modules:
  0.0 130.3 jit_solution(10099925414389207615)
XLA Ops:
  0.7 1.1 copy_bitcast_fusion.2
  1.8 1.6 %collective-permute-start = (bf16[2,128,128]{2,1,0:T(8,128)(2,1)S(1)}, bf16[2,128,128]{2,1,0:T(8,128)(2,1)S(1)}, u32[]{:S(2)}, u32[]{:S(2)}) collective-permute-start(bf16[2,128,128]{2,1,0:T(8,128)(2,1)S(1)} %get-tuple-element.64), channel_id=1, source_target_pairs={{0,2},{2,4},{4,6},{6,0},{1,3},{3,5},{5,7},{7,1},{8,10},{10,12},{12... | collective-permute-start | bytes 196616 | tf_op jit(solution)/shard_map/ppermute | solution.py:423
  3.4 2.8 %collective-permute-start.1 = (bf16[2,128,128]{2,1,0:T(8,128)(2,1)S(1)}, bf16[2,128,128]{2,1,0:T(8,128)(2,1)S(1)}, u32[]{:S(2)}, u32[]{:S(2)}) collective-permute-start(bf16[2,128,128]{2,1,0:T(8,128)(2,1)S(1)} %get-tuple-element.65), channel_id=1, source_target_pairs={{0,4},{2,6},{4,0},{6,2},{1,5},{3,7},{5,1},{7,3},{8,12},{10,14},{12... | collective-permute-start | bytes 196616 | tf_op jit(solution)/shard_map/ppermute | solution.py:423
  6.2 0.4 collective-permute-start.2
  6.7 1.6 %copy.26 = bf16[32,128,128]{2,1,0:T(8,128)(2,1)S(1)} copy(bf16[32,128,128]{2,0,1:T(8,128)(2,1)} %bitcast.75) | data formatting | bytes 2097152 | tf_op jit(solution)/shard_map/transpose | solution.py:447
  8.3 0.4 copy.27
  8.7 1.5 %pad_maximum_fusion = bf16[8,2,4,128,128]{4,3,2,1,0:T(8,128)(2,1)} fusion(bf16[8,1,4,128,128]{4,3,2,1,0:T(8,128)(2,1)S(1)} %bitcast.74, bf16[8,1,4,128,128]{4,3,2,1,0:T(8,128)(2,1)S(1)} %bitcast.73), kind=kLoop, calls=%fused_computation | loop fusion | flops 1048576 | bytes 4194304 | tf_op jit(solution)/shard_map/stack | solution.py:449
  10.3 0.0 collective-permute-done
  10.3 0.0 collective-permute-done.1
  10.3 0.2 collective-permute-done.2
  10.6 0.0 copy-start.12
  10.6 0.0 copy-start.13
  10.6 4.9 %all-to-all-start = ((bf16[8,2,4,128,128]{4,3,2,1,0:T(8,128)(2,1)}), bf16[8,2,4,128,128]{4,3,2,1,0:T(8,128)(2,1)S(1)}, u32[]{:S(2)}, u32[]{:S(2)}) async-start(bf16[8,2,4,128,128]{4,3,2,1,0:T(8,128)(2,1)} %pad_maximum_fusion), calls=%async_computation | async-start | bytes 4194304 | tf_op jit(solution)/shard_map/all_to_all | solution.py:460
  15.5 1.7 %collective-permute-start.3 = (bf16[4,2,128,128]{3,2,1,0:T(8,128)(2,1)S(1)}, bf16[4,2,128,128]{3,2,1,0:T(8,128)(2,1)S(1)}, u32[]{:S(2)}, u32[]{:S(2)}) collective-permute-start(bf16[4,2,128,128]{3,2,1,0:T(8,128)(2,1)S(1)} %pad_maximum_fusion.1.refs_0_), channel_id=1, source_target_pairs={{0,8},{8,0},{16,24},{24,16},{32,40},{40,32},{48,56},{56,48},{64,72... | collective-permute-start | bytes 786440 | tf_op jit(solution)/shard_map/ppermute | solution.py:436
  17.1 2.9 %collective-permute-start.6 = (bf16[4,2,128,128]{3,2,1,0:T(8,128)(2,1)S(1)}, bf16[4,2,128,128]{3,2,1,0:T(8,128)(2,1)S(1)}, u32[]{:S(2)}, u32[]{:S(2)}) collective-permute-start(bf16[4,2,128,128]{3,2,1,0:T(8,128)(2,1)S(1)} %pad_maximum_fusion.1.refs_0_), channel_id=1, source_target_pairs={{0,16},{8,24},{16,32},{24,40},{32,48},{40,56},{48,64},{56,72},{64,... | collective-permute-start | bytes 786440 | tf_op jit(solution)/shard_map/ppermute | solution.py:436
  20.0 1.6 %collective-permute-start.7 = (bf16[4,2,128,128]{3,2,1,0:T(8,128)(2,1)S(1)}, bf16[4,2,128,128]{3,2,1,0:T(8,128)(2,1)S(1)}, u32[]{:S(2)}, u32[]{:S(2)}) collective-permute-start(bf16[4,2,128,128]{3,2,1,0:T(8,128)(2,1)S(1)} %pad_maximum_fusion.1.refs_0_), channel_id=1, source_target_pairs={{0,24},{8,16},{16,40},{24,32},{32,56},{40,48},{48,72},{56,64},{64,... | collective-permute-start | bytes 786440 | tf_op jit(solution)/shard_map/ppermute | solution.py:436
  21.6 0.1 convert_reduce_fusion
  21.8 0.7 select_reduce_fusion.3
  22.5 0.2 select_reduce_fusion
  22.7 0.2 fusion.18
  22.9 0.2 select_reduce_fusion.7
  23.0 0.2 select_reduce_fusion.6
  23.2 1.5 %collective-permute-done.3.refs_1_ = bf16[4,2,128,128]{3,2,1,0:T(8,128)(2,1)S(1)} collective-permute-done((bf16[4,2,128,128]{3,2,1,0:T(8,128)(2,1)S(1)}, bf16[4,2,128,128]{3,2,1,0:T(8,128)(2,1)S(1)}, u32[]{:S(2)}, u32[]{:S(2)}) %collective-permute-start.3) | collective-permute-done | bytes 262176 | tf_op jit(solution)/shard_map/ppermute | solution.py:436
  24.7 0.0 collective-permute-start.5
  24.7 8.6 %collective-permute-done.6.refs_4_ = bf16[4,2,128,128]{3,2,1,0:T(8,128)(2,1)S(1)} collective-permute-done((bf16[4,2,128,128]{3,2,1,0:T(8,128)(2,1)S(1)}, bf16[4,2,128,128]{3,2,1,0:T(8,128)(2,1)S(1)}, u32[]{:S(2)}, u32[]{:S(2)}) %collective-permute-start.6) | collective-permute-done | bytes 262176 | tf_op jit(solution)/shard_map/ppermute | solution.py:436
  33.3 0.0 collective-permute-start.8
  33.3 4.1 %collective-permute-done.7.refs_5_ = bf16[4,2,128,128]{3,2,1,0:T(8,128)(2,1)S(1)} collective-permute-done((bf16[4,2,128,128]{3,2,1,0:T(8,128)(2,1)S(1)}, bf16[4,2,128,128]{3,2,1,0:T(8,128)(2,1)S(1)}, u32[]{:S(2)}, u32[]{:S(2)}) %collective-permute-start.7) | collective-permute-done | bytes 262176 | tf_op jit(solution)/shard_map/ppermute | solution.py:436
  37.4 0.0 collective-permute-start.9
  37.4 0.1 select_reduce_fusion.8
  38.3 0.2 fusion.16
  38.4 0.1 select_reduce_fusion.2
  38.6 0.7 concatenate.3.sc
  39.2 0.0 collective-permute-done.4.refs_2_
  39.2 0.0 collective-permute-done.8.refs_6_
  39.2 0.0 collective-permute-done.9.refs_7_
  39.3 0.7 copy-done.11
  39.9 5.4 %window_keys.1 = (bf16[4096,128]{1,0:T(8,128)(2,1)}, bf16[4096,128]{1,0:T(8,128)(2,1)}, bf16[8,128,512]{2,1,0:T(8,128)(2,1)}, bf16[8,128,512]{2,1,0:T(8,128)(2,1)}, f32[1,512]{1,0:T(1,128)}) custom-call(s32[177]{0:T(256)} %concatenate.3.sc, bf16[4,2,128,128]{3,2,1,0:T(8,128)(2,1)} %copy-done.7, bf16[4,2,128,128]{3,2,1,0:T(8,128)(2,1)} %copy-done.8, ...), custom_call_target="tpu_custom_call" | custom-call | flops 1048576 | bytes 6291456 | tf_op jit(solution)/shard_map/window_keys/pallas_call | solution.py:306
  45.4 0.0 copy-start.1
  45.4 1.2 copy-done.1
  46.6 1.2 copy-done.2
  47.8 1.2 copy-done.3
  49.1 1.2 copy-done.4
  50.3 0.7 copy-done.5
  51.0 40.0 %window_attention.1 = (bf16[8,2,4,128,128]{4,3,2,1,0:T(8,128)(2,1)}, bf16[2,2,4,2,128,128]{5,4,3,2,1,0:T(8,128)(2,1)S(1)}, bf16[2,2,4,2,128,128]{5,4,3,2,1,0:T(8,128)(2,1)}) custom-call(s32[177]{0:T(256)S(1)} %copy-done, f32[1,512]{1,0:T(1,128)S(1)} %copy-done.5, bf16[8,2,4,128,128]{4,3,2,1,0:T(8,128)(2,1)S(1)} %all-to-all-done.rows_ref, ...), custom_call_target="tpu_custom_call" | custom-call | flops 21474836480 | bytes 6291456 | tf_op jit(solution)/shard_map/window_attention/pallas_call | solution.py:306
  91.0 0.8 collective-permute-start.10
  91.7 4.8 %all-to-all-start.1 = ((bf16[8,2,4,128,128]{4,3,2,1,0:T(8,128)(2,1)}), bf16[8,2,4,128,128]{4,3,2,1,0:T(8,128)(2,1)S(1)}, u32[]{:S(2)}, u32[]{:S(2)}) async-start(bf16[8,2,4,128,128]{4,3,2,1,0:T(8,128)(2,1)} %get-tuple-element.25), calls=%async_computation.1 | async-start | bytes 4194304 | tf_op jit(solution)/shard_map/all_to_all | solution.py:472
  96.6 0.0 collective-permute-done.10
  96.6 1.3 %fusion.4 = (bf16[4,2,128,128]{3,2,1,0:T(8,128)(2,1)S(1)}, bf16[4,2,128,128]{3,2,1,0:T(8,128)(2,1)S(1)}, bf16[4,2,128,128]{3,2,1,0:T(8,128)(2,1)S(1)}) fusion(bf16[2,2,4,2,128,128]{5,4,3,2,1,0:T(8,128)(2,1)} %collective-permute-done.10, bf16[2,2,4,2,128,128]{5,4,3,2,1,0:T(8,128)(2,1)S(1)} %get-tuple-element.26), kind=kLoop, calls=%fused_computation.20 | loop fusion | flops 1572864 | bytes 2359296 | tf_op jit(solution)/shard_map/convert_element_type | solution.py:419
  97.9 0.1 collective-permute-start.11
  98.0 1.0 collective-permute-start.12
  99.1 0.5 collective-permute-start.13
  99.6 12.4 %collective-permute-done.11 = bf16[4,2,128,128]{3,2,1,0:T(8,128)(2,1)S(1)} collective-permute-done((bf16[4,2,128,128]{3,2,1,0:T(8,128)(2,1)S(1)}, bf16[4,2,128,128]{3,2,1,0:T(8,128)(2,1)S(1)}, u32[]{:S(2)}, u32[]{:S(2)}) %collective-permute-start.11) | collective-permute-done | bytes 262176 | tf_op jit(solution)/shard_map/ppermute | solution.py:436
  112.0 1.6 %collective-permute-done.13 = bf16[4,2,128,128]{3,2,1,0:T(8,128)(2,1)S(1)} collective-permute-done((bf16[4,2,128,128]{3,2,1,0:T(8,128)(2,1)S(1)}, bf16[4,2,128,128]{3,2,1,0:T(8,128)(2,1)S(1)}, u32[]{:S(2)}, u32[]{:S(2)}) %collective-permute-start.13) | collective-permute-done | bytes 262176 | tf_op jit(solution)/shard_map/ppermute | solution.py:436
  113.6 1.1 fusion.2
  114.7 0.4 collective-permute-start.14
  115.2 2.6 %collective-permute-start.15 = (bf16[2,128,128]{2,1,0:T(8,128)(2,1)S(1)}, bf16[2,128,128]{2,1,0:T(8,128)(2,1)S(1)}, u32[]{:S(2)}, u32[]{:S(2)}) collective-permute-start(bf16[2,128,128]{2,1,0:T(8,128)(2,1)S(1)} %get-tuple-element.62), channel_id=1, source_target_pairs={{0,4},{2,6},{4,0},{6,2},{1,5},{3,7},{5,1},{7,3},{8,12},{10,14},{12... | collective-permute-start | bytes 196616 | tf_op jit(solution)/shard_map/ppermute | solution.py:423
  117.7 1.8 %collective-permute-start.16 = (bf16[2,128,128]{2,1,0:T(8,128)(2,1)S(1)}, bf16[2,128,128]{2,1,0:T(8,128)(2,1)S(1)}, u32[]{:S(2)}, u32[]{:S(2)}) collective-permute-start(bf16[2,128,128]{2,1,0:T(8,128)(2,1)S(1)} %get-tuple-element.61), channel_id=1, source_target_pairs={{0,2},{2,4},{4,6},{6,0},{1,3},{3,5},{5,7},{7,1},{8,10},{10,12},{12... | collective-permute-start | bytes 196616 | tf_op jit(solution)/shard_map/ppermute | solution.py:423
  119.5 4.6 %collective-permute-done.14 = bf16[2,128,128]{2,1,0:T(8,128)(2,1)S(1)} collective-permute-done((bf16[2,128,128]{2,1,0:T(8,128)(2,1)S(1)}, bf16[2,128,128]{2,1,0:T(8,128)(2,1)S(1)}, u32[]{:S(2)}, u32[]{:S(2)}) %collective-permute-start.14) | collective-permute-done | bytes 65568 | tf_op jit(solution)/shard_map/ppermute | solution.py:423
  124.2 1.0 collective-permute-done.15
  125.3 0.8 copy.30
  126.1 0.8 copy.31
  126.8 0.1 fusion.31
  127.0 1.6 %copy.36 = bf16[32,128,128]{2,0,1:T(8,128)(2,1)} copy(bf16[32,128,128]{2,1,0:T(8,128)(2,1)S(1)} %bitcast.72) | data formatting | bytes 2097152 | tf_op jit(solution)/shard_map/reshape;squeeze | solution.py:475
  128.6 1.6 %copy.37 = bf16[32,128,128]{2,0,1:T(8,128)(2,1)} copy(bf16[32,128,128]{2,1,0:T(8,128)(2,1)S(1)} %bitcast.71) | data formatting | bytes 2097152 | tf_op jit(solution)/shard_map/reshape;squeeze | solution.py:475
  (40 shorter events, 0.3 us)
Async XLA Ops:
  0.6 7.7 %copy-start.6 = (bf16[128,32,128]{2,1,0:T(8,128)(2,1)S(1)}, bf16[128,32,128]{2,1,0:T(8,128)(2,1)}, u32[]{:S(2)}) copy-start(bf16[128,32,128]{2,1,0:T(8,128)(2,1)} %param.9) | copy-start | bytes 3145732
  1.8 8.4 %collective-permute-start = (bf16[2,128,128]{2,1,0:T(8,128)(2,1)S(1)}, bf16[2,128,128]{2,1,0:T(8,128)(2,1)S(1)}, u32[]{:S(2)}, u32[]{:S(2)}) collective-permute-start(bf16[2,128,128]{2,1,0:T(8,128)(2,1)S(1)} %get-tuple-element.64), channel_id=1, source_target_pairs={{0,2},{2,4},{4,6},{6,0},{1,3},{3,5},{5,7},{7,1},{8,10},{10,12},{12... | collective-permute-start | bytes 196616 | tf_op jit(solution)/shard_map/ppermute | solution.py:423
  3.4 6.9 %collective-permute-start.1 = (bf16[2,128,128]{2,1,0:T(8,128)(2,1)S(1)}, bf16[2,128,128]{2,1,0:T(8,128)(2,1)S(1)}, u32[]{:S(2)}, u32[]{:S(2)}) collective-permute-start(bf16[2,128,128]{2,1,0:T(8,128)(2,1)S(1)} %get-tuple-element.65), channel_id=1, source_target_pairs={{0,4},{2,6},{4,0},{6,2},{1,5},{3,7},{5,1},{7,3},{8,12},{10,14},{12... | collective-permute-start | bytes 196616 | tf_op jit(solution)/shard_map/ppermute | solution.py:423
  6.2 4.3 %collective-permute-start.2 = (bf16[2,128,128]{2,1,0:T(8,128)(2,1)S(1)}, bf16[2,128,128]{2,1,0:T(8,128)(2,1)S(1)}, u32[]{:S(2)}, u32[]{:S(2)}) collective-permute-start(bf16[2,128,128]{2,1,0:T(8,128)(2,1)S(1)} %get-tuple-element.66), channel_id=1, source_target_pairs={{0,6},{2,0},{4,2},{6,4},{1,7},{3,1},{5,3},{7,5},{8,14},{10,8},{12,... | collective-permute-start | bytes 196616 | tf_op jit(solution)/shard_map/ppermute | solution.py:423
  10.5 11.1 %copy-start.7 = (bf16[4,2,128,128]{3,2,1,0:T(8,128)(2,1)}, bf16[4,2,128,128]{3,2,1,0:T(8,128)(2,1)S(1)}, u32[]{:S(2)}) copy-start(bf16[4,2,128,128]{3,2,1,0:T(8,128)(2,1)S(1)} %pad_maximum_fusion.1.refs_0_) | copy-start | bytes 786436
  10.6 11.1 %copy-start.12 = (s32[256,128]{1,0:T(8,128)S(1)}, s32[256,128]{1,0:T(8,128)}, u32[]{:S(2)}) copy-start(s32[256,128]{1,0:T(8,128)} %param.10) | copy-start | bytes 393220
  10.6 11.2 %copy-start.13 = (s32[256]{0:T(256)S(1)}, s32[256]{0:T(256)}, u32[]{:S(2)}) copy-start(s32[256]{0:T(256)} %param.11) | copy-start | bytes 3076
  10.6 34.8 %all-to-all-start = ((bf16[8,2,4,128,128]{4,3,2,1,0:T(8,128)(2,1)}), bf16[8,2,4,128,128]{4,3,2,1,0:T(8,128)(2,1)S(1)}, u32[]{:S(2)}, u32[]{:S(2)}) async-start(bf16[8,2,4,128,128]{4,3,2,1,0:T(8,128)(2,1)} %pad_maximum_fusion), calls=%async_computation | async-start | bytes 4194304 | tf_op jit(solution)/shard_map/all_to_all | solution.py:460
  15.5 9.2 %collective-permute-start.3 = (bf16[4,2,128,128]{3,2,1,0:T(8,128)(2,1)S(1)}, bf16[4,2,128,128]{3,2,1,0:T(8,128)(2,1)S(1)}, u32[]{:S(2)}, u32[]{:S(2)}) collective-permute-start(bf16[4,2,128,128]{3,2,1,0:T(8,128)(2,1)S(1)} %pad_maximum_fusion.1.refs_0_), channel_id=1, source_target_pairs={{0,8},{8,0},{16,24},{24,16},{32,40},{40,32},{48,56},{56,48},{64,72... | collective-permute-start | bytes 786440 | tf_op jit(solution)/shard_map/ppermute | solution.py:436
  17.1 16.1 %collective-permute-start.6 = (bf16[4,2,128,128]{3,2,1,0:T(8,128)(2,1)S(1)}, bf16[4,2,128,128]{3,2,1,0:T(8,128)(2,1)S(1)}, u32[]{:S(2)}, u32[]{:S(2)}) collective-permute-start(bf16[4,2,128,128]{3,2,1,0:T(8,128)(2,1)S(1)} %pad_maximum_fusion.1.refs_0_), channel_id=1, source_target_pairs={{0,16},{8,24},{16,32},{24,40},{32,48},{40,56},{48,64},{56,72},{64,... | collective-permute-start | bytes 786440 | tf_op jit(solution)/shard_map/ppermute | solution.py:436
  20.0 17.3 %collective-permute-start.7 = (bf16[4,2,128,128]{3,2,1,0:T(8,128)(2,1)S(1)}, bf16[4,2,128,128]{3,2,1,0:T(8,128)(2,1)S(1)}, u32[]{:S(2)}, u32[]{:S(2)}) collective-permute-start(bf16[4,2,128,128]{3,2,1,0:T(8,128)(2,1)S(1)} %pad_maximum_fusion.1.refs_0_), channel_id=1, source_target_pairs={{0,24},{8,16},{16,40},{24,32},{32,56},{40,48},{48,72},{56,64},{64,... | collective-permute-start | bytes 786440 | tf_op jit(solution)/shard_map/ppermute | solution.py:436
  21.6 17.6 %collective-permute-start.4 = (bf16[4,2,128,128]{3,2,1,0:T(8,128)(2,1)S(1)}, bf16[4,2,128,128]{3,2,1,0:T(8,128)(2,1)S(1)}, u32[]{:S(2)}, u32[]{:S(2)}) collective-permute-start(bf16[4,2,128,128]{3,2,1,0:T(8,128)(2,1)S(1)} %pad_maximum_fusion.1.refs_0_), channel_id=1, source_target_pairs={{0,1},{1,0},{2,3},{3,2},{4,5},{5,4},{6,7},{7,6},{8,9},{9,8},{10,11... | collective-permute-start | bytes 786440 | tf_op jit(solution)/shard_map/ppermute | solution.py:427
  24.7 14.5 %copy-start.8 = (bf16[4,2,128,128]{3,2,1,0:T(8,128)(2,1)}, bf16[4,2,128,128]{3,2,1,0:T(8,128)(2,1)S(1)}, u32[]{:S(2)}) copy-start(bf16[4,2,128,128]{3,2,1,0:T(8,128)(2,1)S(1)} %collective-permute-done.3.refs_1_) | copy-start | bytes 786436
  24.7 14.5 %collective-permute-start.5 = (bf16[4,2,128,128]{3,2,1,0:T(8,128)(2,1)S(1)}, bf16[4,2,128,128]{3,2,1,0:T(8,128)(2,1)}, u32[]{:S(2)}, u32[]{:S(2)}) collective-permute-start(bf16[4,2,128,128]{3,2,1,0:T(8,128)(2,1)S(1)} %collective-permute-done.3.refs_1_), channel_id=1, source_target_pairs={{0,1},{1,0},{2,3},{3,2},{4,5},{5,4},{6,7},{7,6},{8,9},{9,8},{10,11... | collective-permute-start | bytes 786440 | tf_op jit(solution)/shard_map/ppermute | solution.py:427
  33.3 6.0 %copy-start.9 = (bf16[4,2,128,128]{3,2,1,0:T(8,128)(2,1)}, bf16[4,2,128,128]{3,2,1,0:T(8,128)(2,1)S(1)}, u32[]{:S(2)}) copy-start(bf16[4,2,128,128]{3,2,1,0:T(8,128)(2,1)S(1)} %collective-permute-done.6.refs_4_) | copy-start | bytes 786436
  33.3 5.9 %collective-permute-start.8 = (bf16[4,2,128,128]{3,2,1,0:T(8,128)(2,1)S(1)}, bf16[4,2,128,128]{3,2,1,0:T(8,128)(2,1)}, u32[]{:S(2)}, u32[]{:S(2)}) collective-permute-start(bf16[4,2,128,128]{3,2,1,0:T(8,128)(2,1)S(1)} %collective-permute-done.6.refs_4_), channel_id=1, source_target_pairs={{0,1},{1,0},{2,3},{3,2},{4,5},{5,4},{6,7},{7,6},{8,9},{9,8},{10,11... | collective-permute-start | bytes 786440 | tf_op jit(solution)/shard_map/ppermute | solution.py:427
  37.4 1.9 %copy-start.10 = (bf16[4,2,128,128]{3,2,1,0:T(8,128)(2,1)}, bf16[4,2,128,128]{3,2,1,0:T(8,128)(2,1)S(1)}, u32[]{:S(2)}) copy-start(bf16[4,2,128,128]{3,2,1,0:T(8,128)(2,1)S(1)} %collective-permute-done.7.refs_5_) | copy-start | bytes 786436
  37.4 1.9 %collective-permute-start.9 = (bf16[4,2,128,128]{3,2,1,0:T(8,128)(2,1)S(1)}, bf16[4,2,128,128]{3,2,1,0:T(8,128)(2,1)}, u32[]{:S(2)}, u32[]{:S(2)}) collective-permute-start(bf16[4,2,128,128]{3,2,1,0:T(8,128)(2,1)S(1)} %collective-permute-done.7.refs_5_), channel_id=1, source_target_pairs={{0,1},{1,0},{2,3},{3,2},{4,5},{5,4},{6,7},{7,6},{8,9},{9,8},{10,11... | collective-permute-start | bytes 786440 | tf_op jit(solution)/shard_map/ppermute | solution.py:427
  39.2 6.1 %copy-start = (s32[177]{0:T(256)S(1)}, s32[177]{0:T(256)}, u32[]{:S(2)}) copy-start(s32[177]{0:T(256)} %concatenate.3.sc) | copy-start | bytes 2128
  39.2 0.7 copy-start.11
  45.4 1.2 copy-start.1
  46.6 1.2 copy-start.2
  47.8 1.2 copy-start.3
  49.0 1.2 copy-start.4
  50.3 0.7 copy-start.5
  91.0 5.6 %collective-permute-start.10 = (bf16[2,2,4,2,128,128]{5,4,3,2,1,0:T(8,128)(2,1)}, bf16[2,2,4,2,128,128]{5,4,3,2,1,0:T(8,128)(2,1)}, u32[]{:S(2)}, u32[]{:S(2)}) collective-permute-start(bf16[2,2,4,2,128,128]{5,4,3,2,1,0:T(8,128)(2,1)} %get-tuple-element.27), channel_id=1, source_target_pairs={{0,1},{1,0},{2,3},{3,2},{4,5},{5,4},{6,7},{7,6},{8,9},{9,8},{10,11... | collective-permute-start | bytes 3145736 | tf_op jit(solution)/shard_map/ppermute | solution.py:427
  91.7 35.1 %all-to-all-start.1 = ((bf16[8,2,4,128,128]{4,3,2,1,0:T(8,128)(2,1)}), bf16[8,2,4,128,128]{4,3,2,1,0:T(8,128)(2,1)S(1)}, u32[]{:S(2)}, u32[]{:S(2)}) async-start(bf16[8,2,4,128,128]{4,3,2,1,0:T(8,128)(2,1)} %get-tuple-element.25), calls=%async_computation.1 | async-start | bytes 4194304 | tf_op jit(solution)/shard_map/all_to_all | solution.py:472
  97.9 14.1 %collective-permute-start.11 = (bf16[4,2,128,128]{3,2,1,0:T(8,128)(2,1)S(1)}, bf16[4,2,128,128]{3,2,1,0:T(8,128)(2,1)S(1)}, u32[]{:S(2)}, u32[]{:S(2)}) collective-permute-start(bf16[4,2,128,128]{3,2,1,0:T(8,128)(2,1)S(1)} %get-tuple-element.49), channel_id=1, source_target_pairs={{0,8},{8,0},{16,24},{24,16},{32,40},{40,32},{48,56},{56,48},{64,72... | collective-permute-start | bytes 786440 | tf_op jit(solution)/shard_map/ppermute | solution.py:436
  98.0 14.0 %collective-permute-start.12 = (bf16[4,2,128,128]{3,2,1,0:T(8,128)(2,1)S(1)}, bf16[4,2,128,128]{3,2,1,0:T(8,128)(2,1)S(1)}, u32[]{:S(2)}, u32[]{:S(2)}) collective-permute-start(bf16[4,2,128,128]{3,2,1,0:T(8,128)(2,1)S(1)} %get-tuple-element.51), channel_id=1, source_target_pairs={{0,240},{8,248},{16,0},{24,8},{32,16},{40,24},{48,32},{56,40},{64,... | collective-permute-start | bytes 786440 | tf_op jit(solution)/shard_map/ppermute | solution.py:436
  99.1 14.5 %collective-permute-start.13 = (bf16[4,2,128,128]{3,2,1,0:T(8,128)(2,1)S(1)}, bf16[4,2,128,128]{3,2,1,0:T(8,128)(2,1)S(1)}, u32[]{:S(2)}, u32[]{:S(2)}) collective-permute-start(bf16[4,2,128,128]{3,2,1,0:T(8,128)(2,1)S(1)} %get-tuple-element.50), channel_id=1, source_target_pairs={{0,248},{8,240},{16,8},{24,0},{32,24},{40,16},{48,40},{56,32},{64,... | collective-permute-start | bytes 786440 | tf_op jit(solution)/shard_map/ppermute | solution.py:436
  114.7 9.4 %collective-permute-start.14 = (bf16[2,128,128]{2,1,0:T(8,128)(2,1)S(1)}, bf16[2,128,128]{2,1,0:T(8,128)(2,1)S(1)}, u32[]{:S(2)}, u32[]{:S(2)}) collective-permute-start(bf16[2,128,128]{2,1,0:T(8,128)(2,1)S(1)} %get-tuple-element.60), channel_id=1, source_target_pairs={{0,6},{2,0},{4,2},{6,4},{1,7},{3,1},{5,3},{7,5},{8,14},{10,8},{12,... | collective-permute-start | bytes 196616 | tf_op jit(solution)/shard_map/ppermute | solution.py:423
  115.2 10.0 %collective-permute-start.15 = (bf16[2,128,128]{2,1,0:T(8,128)(2,1)S(1)}, bf16[2,128,128]{2,1,0:T(8,128)(2,1)S(1)}, u32[]{:S(2)}, u32[]{:S(2)}) collective-permute-start(bf16[2,128,128]{2,1,0:T(8,128)(2,1)S(1)} %get-tuple-element.62), channel_id=1, source_target_pairs={{0,4},{2,6},{4,0},{6,2},{1,5},{3,7},{5,1},{7,3},{8,12},{10,14},{12... | collective-permute-start | bytes 196616 | tf_op jit(solution)/shard_map/ppermute | solution.py:423
  117.7 7.4 %collective-permute-start.16 = (bf16[2,128,128]{2,1,0:T(8,128)(2,1)S(1)}, bf16[2,128,128]{2,1,0:T(8,128)(2,1)S(1)}, u32[]{:S(2)}, u32[]{:S(2)}) collective-permute-start(bf16[2,128,128]{2,1,0:T(8,128)(2,1)S(1)} %get-tuple-element.61), channel_id=1, source_target_pairs={{0,2},{2,4},{4,6},{6,0},{1,3},{3,5},{5,7},{7,1},{8,10},{10,12},{12... | collective-permute-start | bytes 196616 | tf_op jit(solution)/shard_map/ppermute | solution.py:423
where the time goes:
time: 132 us; the launch traced here: 130 us
  Pallas kernels  45.4 us (34%)
  waiting for transfers between devices  34.1 us (26%)
  starting transfers between devices  27.8 us (21%)
  local copies, waits for them, and re-layouts  15.1 us (11%)
  other arithmetic  6.16 us (5%)
  between operations  1.68 us (1%)
    pallas_call x2, Pallas kernels, call(): pl.pallas_call(kernel, out_shape=out_shape, in_specs=[pl.BlockSpec(memory...  45.4 us
    ppermute x6, waiting for transfers between devices, to_group(): return lax.ppermute(block, ('outer', 'y'), route)  28.2 us
    ppermute x6, starting transfers between devices, to_x(): return lax.ppermute(block, 'x', [(i, (i + step) % N_X) for i in range(N_X)])  9.61 us
    unnamed x30, local copies, waits for them, and re-layouts  7.79 us
    ppermute x6, starting transfers between devices, to_group(): return lax.ppermute(block, ('outer', 'y'), route)  7.75 us
    ppermute x6, waiting for transfers between devices, to_x(): return lax.ppermute(block, 'x', [(i, (i + step) % N_X) for i in range(N_X)])  5.91 us
    all_to_all x1, starting transfers between devices, on_device(): rows = exchange(rows, QUERY_AXES)  4.85 us
    all_to_all x1, starting transfers between devices, on_device(): home = exchange(rows, QUERY_AXES)  4.84 us
  transfers between devices with their start and end apart: 19, of which 8 were waited for; matrix products, arithmetic and copies ran while one was open for 8% of the time, Pallas kernels for 4%

commit v1 on v0

--- a/solution.py
+++ b/solution.py
@@ -104,7 +104,8 @@
 
 
 def prepare(sc, *refs):
-    pieces, (kc, vc, kt, vt, long_ref, stage, kf, vf, sems) = refs[:PIECES], refs[PIECES:]
+    pieces, out_refs, long_ref = refs[:PIECES], refs[PIECES : PIECES + 4], refs[PIECES + 4]
+    kc, vc, kt, vt, longs, stage, kf, vf, sems, out_sems = refs[PIECES + 5 :]
     spans = up(sc[REACH + sc[TILE_COUNT] - 1], SPAN)
     copies = [
         pltpu.make_async_copy(ref, stage.at[pl.ds(p * N_X, N_X)], sems.at[p])
@@ -136,13 +137,21 @@
         vt[n] = vals.T
         return jnp.maximum(longest, square(keys))
 
-    long_ref[...] = lax.fori_loop(0, spans, turn, jnp.zeros((1, SPAN), F32))
+    longs[...] = lax.fori_loop(0, spans, turn, jnp.zeros((1, SPAN), F32))
+    out_copies = [
+        pltpu.make_async_copy(held, ref, out_sems.at[n])
+        for n, (held, ref) in enumerate(zip((kc, vc, kt, vt, longs), (*out_refs, long_ref)))
+    ]
+    for copy in out_copies:
+        copy.start()
+    for copy in out_copies:
+        copy.wait()
 
 
 def attend(sc, long_ref, rows_ref, *refs):
     keys_refs, (out_ref, *term_refs), scratch = refs[:4], refs[4:7], refs[7:]
     raw, kc, vc, kt, vt, qf, gf, thr, limits, qt, gt, ot, dqt = scratch[:13]
-    wb, wn, db, dk, dv, terms, sems, out_sems = scratch[13:]
+    wb, wn, db, dk, dv, tops, terms, sems, out_sems = scratch[13:]
     slot = slots()
     tiles = sc[TILE_COUNT]
 
@@ -185,34 +194,33 @@
     longest_row = jnp.max(lax.fori_loop(0, tiles, turn, jnp.zeros((1, LANES), F32)))
     safe = longest_row * longest * BASE_TWO ** 2 <= SAFE ** 2
 
+    def span_rows(n):
+        return pl.ds(pl.multiple_of(n * SPAN, SPAN), SPAN)
+
+    def scores(i, n):
+        s = jnp.dot(kc[span_rows(n), :], qt[i], preferred_element_type=F32)
+        return shown(s, n * SPAN, limits[i])
+
+    def weigh(i, n):
+        w = jnp.exp2(scores(i, n) * BASE_TWO - tops[i])
+        low = w.astype(BF16)
+        wb[span_rows(n), :] = low
+        wn[...] = low
+        return fold(jnp.sum, w)
+
     @pl.loop(0, tiles)
     def _(i):
+        top = lax.fori_loop(
+            0,
+            jnp.where(safe, 0, up(sc[REACH + i], SPAN)),
+            lambda n, top: jnp.maximum(top, fold(jnp.max, scores(i, n))),
+            jnp.full((8, LANES), jnp.where(safe, 0.0, FLOOR), F32),
+        )
+        tops[i] = jnp.max(top, axis=0, keepdims=True) * BASE_TWO
+
+    def attend_tile(i, total):
         rows = tile_rows(i)
         count = up(sc[REACH + i], SPAN)
-        limit = limits[i]
-        q_turn = qt[i]
-
-        def span_rows(n):
-            return pl.ds(pl.multiple_of(n * SPAN, SPAN), SPAN)
-
-        def scores(n):
-            s = jnp.dot(kc[span_rows(n), :], q_turn, preferred_element_type=F32)
-            return shown(s, n * SPAN, limit)
-
-        top = lax.fori_loop(
-            0,
-            jnp.where(safe, 0, count),
-            lambda n, top: jnp.maximum(top, fold(jnp.max, scores(n))),
-            jnp.full((8, LANES), jnp.where(safe, 0.0, FLOOR), F32),
-        )
-        top = jnp.max(top, axis=0, keepdims=True) * BASE_TWO
-
-        def weigh(n):
-            w = jnp.exp2(scores(n) * BASE_TWO - top)
-            low = w.astype(BF16)
-            wb[span_rows(n), :] = low
-            wn[...] = low
-            return fold(jnp.sum, w)
 
         def mix(n):
             return jnp.dot(vt[n], wn[...], preferred_element_type=F32)
@@ -220,9 +228,8 @@
         def step(n, carry):
             total, acc = carry
             acc = acc + mix(n - 1)
-            return total + weigh(n), acc
-
-        total = weigh(0)
+            return total + weigh(i, n), acc
+
         total, acc = lax.fori_loop(1, count, step, (total, jnp.zeros((WIDTH, LANES), F32)))
         acc = acc + mix(count - 1)
         total = jnp.sum(total, axis=0, keepdims=True)
@@ -259,6 +266,9 @@
         acc = lax.fori_loop(1, count, step_back, jnp.zeros((WIDTH, LANES), F32))
         acc = mix_back(count - 1, acc)
         dqt[i] = (acc * (inverse * SCALE)).astype(BF16)
+        return weigh(jnp.minimum(i + 1, tiles - 1), 0)
+
+    lax.fori_loop(0, tiles, attend_tile, weigh(0, 0))
 
     out_copies = [
         pltpu.make_async_copy(terms.at[far], term_refs[far], out_sems.at[far]) for far in range(2)
@@ -328,15 +338,19 @@
             shape(TURNED_KEYS, BF16),
             shape((1, SPAN), F32),
         ),
-        pltpu.VMEM,
+        pltpu.HBM,
         [
+            *[pltpu.VMEM(KEYS, BF16)] * 2,
+            *[pltpu.VMEM(TURNED_KEYS, BF16)] * 2,
+            pltpu.VMEM((1, SPAN), F32),
             pltpu.VMEM((WINDOW, 2, SLOTS, WIDTH), BF16),
             PACKING_KEYS,
             PACKING_KEYS,
             pltpu.SemaphoreType.DMA((PIECES,)),
+            pltpu.SemaphoreType.DMA((5,)),
         ],
         1 << 20,
-        56,
+        42,
         "window_keys",
     )
 
@@ -362,6 +376,7 @@
             pltpu.VMEM((SPAN, LANES), BF16),
             pltpu.VMEM((SPAN, LANES), BF16),
             *[PACKING_KEYS] * 2,
+            pltpu.VMEM((TILES, 1, LANES), F32),
             pltpu.VMEM((2, *terms.shape), BF16),
             pltpu.SemaphoreType.DMA((5,)),
             pltpu.SemaphoreType.DMA((4,)),
@@ -468,15 +483,17 @@
         to_group(term(1, 1), -1, 1),
     )
     grads = [to_x(sums[k], -k) if k else sums[0] for k in range(N_X)]
-    grads = jnp.stack([lax.select_n((h - x) % N_X, *grads) for h in range(N_X)])
     home = exchange(rows, QUERY_AXES)
 
     def by_slot(a):
         return a.reshape(HEADS_Q, SLOTS, WIDTH).transpose(1, 0, 2)
 
+    output, query_gradient = by_slot(home[:, 0]), by_slot(home[:, 1])
+    output, query_gradient, grads = lax.optimization_barrier((output, query_gradient, grads))
+    grads = jnp.stack([lax.select_n((h - x) % N_X, *grads) for h in range(N_X)])
     return (
-        by_slot(home[:, 0]),
-        by_slot(home[:, 1]),
+        output,
+        query_gradient,
         grads[:, 0].transpose(1, 0, 2),
         grads[:, 1].transpose(1, 0, 2),
     )

time: 132 us -> 128 us (0.970)
  the two profiles are of different devices: /device:TPU:2 before, /device:TPU:208 now
where the time goes in v1:
time: 128 us; the launch traced here: 126 us
  starting transfers between devices  37 us (29%)
  Pallas kernels  31 us (24%)
  waiting for transfers between devices  30.5 us (24%)
  local copies, waits for them, and re-layouts  18.4 us (14%)
  other arithmetic  7.18 us (6%)
  between operations  1.68 us (1%)
    pallas_call x2, Pallas kernels, call(): pl.pallas_call(kernel, out_shape=out_shape, in_specs=[pl.BlockSpec(memory...  31 us
    ppermute x6, waiting for transfers between devices, to_group(): return lax.ppermute(block, ('outer', 'y'), route)  26.7 us
    ppermute x6, starting transfers between devices, to_group(): return lax.ppermute(block, ('outer', 'y'), route)  18.8 us
    unnamed x26, local copies, waits for them, and re-layouts  11.7 us
    ppermute x6, starting transfers between devices, to_x(): return lax.ppermute(block, 'x', [(i, (i + step) % N_X) for i in range(N_X)])  10.4 us
    all_to_all x1, starting transfers between devices, on_device(): rows = exchange(rows, QUERY_AXES)  3.75 us
    all_to_all x1, starting transfers between devices, on_device(): home = exchange(rows, QUERY_AXES)  3.6 us
    convert_element_type x2, other arithmetic, total(): functools.reduce(jnp.add, [a.astype(F32) for a in parts]).astype(BF16)  3.49 us
  transfers between devices with their start and end apart: 19, of which 9 were waited for; matrix products, arithmetic and copies ran while one was open for 10% of the time, Pallas kernels for 3%

profile of v1, /device:TPU:208, one launch (start us, length us, event | category | flops | bytes accessed | tf_op | source)
XLA Modules:
  0.0 125.8 jit_solution(9090957034797654882)
XLA Ops:
  0.7 1.1 copy_bitcast_fusion.2
  1.8 1.6 %collective-permute-start = (bf16[2,128,128]{2,1,0:T(8,128)(2,1)S(1)}, bf16[2,128,128]{2,1,0:T(8,128)(2,1)S(1)}, u32[]{:S(2)}, u32[]{:S(2)}) collective-permute-start(bf16[2,128,128]{2,1,0:T(8,128)(2,1)S(1)} %get-tuple-element.77), channel_id=1, source_target_pairs={{0,2},{2,4},{4,6},{6,0},{1,3},{3,5},{5,7},{7,1},{8,10},{10,12},{12... | collective-permute-start | bytes 196616 | tf_op jit(solution)/shard_map/ppermute | solution.py:438
  3.4 2.7 %collective-permute-start.1 = (bf16[2,128,128]{2,1,0:T(8,128)(2,1)S(1)}, bf16[2,128,128]{2,1,0:T(8,128)(2,1)S(1)}, u32[]{:S(2)}, u32[]{:S(2)}) collective-permute-start(bf16[2,128,128]{2,1,0:T(8,128)(2,1)S(1)} %get-tuple-element.78), channel_id=1, source_target_pairs={{0,4},{2,6},{4,0},{6,2},{1,5},{3,7},{5,1},{7,3},{8,12},{10,14},{12... | collective-permute-start | bytes 196616 | tf_op jit(solution)/shard_map/ppermute | solution.py:438
  6.1 1.4 %collective-permute-start.2 = (bf16[2,128,128]{2,1,0:T(8,128)(2,1)S(1)}, bf16[2,128,128]{2,1,0:T(8,128)(2,1)S(1)}, u32[]{:S(2)}, u32[]{:S(2)}) collective-permute-start(bf16[2,128,128]{2,1,0:T(8,128)(2,1)S(1)} %get-tuple-element.79), channel_id=1, source_target_pairs={{0,6},{2,0},{4,2},{6,4},{1,7},{3,1},{5,3},{7,5},{8,14},{10,8},{12,... | collective-permute-start | bytes 196616 | tf_op jit(solution)/shard_map/ppermute | solution.py:438
  7.6 1.6 %copy.26 = bf16[32,128,128]{2,1,0:T(8,128)(2,1)S(1)} copy(bf16[32,128,128]{2,0,1:T(8,128)(2,1)} %bitcast.67) | data formatting | bytes 2097152 | tf_op jit(solution)/shard_map/transpose | solution.py:462
  9.2 0.4 copy.27
  9.6 1.5 %pad_maximum_fusion = bf16[8,2,4,128,128]{4,3,2,1,0:T(8,128)(2,1)} fusion(bf16[8,1,4,128,128]{4,3,2,1,0:T(8,128)(2,1)S(1)} %bitcast.66, bf16[8,1,4,128,128]{4,3,2,1,0:T(8,128)(2,1)S(1)} %bitcast.65), kind=kLoop, calls=%fused_computation | loop fusion | flops 1048576 | bytes 4194304 | tf_op jit(solution)/shard_map/stack | solution.py:464
  11.2 0.0 copy-start.10
  11.2 0.0 copy-start.11
  11.2 3.7 %all-to-all-start = ((bf16[8,2,4,128,128]{4,3,2,1,0:T(8,128)(2,1)}), bf16[8,2,4,128,128]{4,3,2,1,0:T(8,128)(2,1)S(1)}, u32[]{:S(2)}, u32[]{:S(2)}) async-start(bf16[8,2,4,128,128]{4,3,2,1,0:T(8,128)(2,1)} %pad_maximum_fusion), calls=%async_computation | async-start | bytes 4194304 | tf_op jit(solution)/shard_map/all_to_all | solution.py:475
  15.0 1.4 %collective-permute-start.3 = (bf16[4,2,128,128]{3,2,1,0:T(8,128)(2,1)S(1)}, bf16[4,2,128,128]{3,2,1,0:T(8,128)(2,1)S(1)}, u32[]{:S(2)}, u32[]{:S(2)}) collective-permute-start(bf16[4,2,128,128]{3,2,1,0:T(8,128)(2,1)S(1)} %pad_maximum_fusion.1.refs_0_), channel_id=1, source_target_pairs={{0,8},{8,0},{16,24},{24,16},{32,40},{40,32},{48,56},{56,48},{64,72... | collective-permute-start | bytes 786440 | tf_op jit(solution)/shard_map/ppermute | solution.py:451
  16.4 1.1 collective-permute-start.6
  17.5 1.6 %collective-permute-start.7 = (bf16[4,2,128,128]{3,2,1,0:T(8,128)(2,1)S(1)}, bf16[4,2,128,128]{3,2,1,0:T(8,128)(2,1)S(1)}, u32[]{:S(2)}, u32[]{:S(2)}) collective-permute-start(bf16[4,2,128,128]{3,2,1,0:T(8,128)(2,1)S(1)} %pad_maximum_fusion.1.refs_0_), channel_id=1, source_target_pairs={{0,24},{8,16},{16,40},{24,32},{32,56},{40,48},{48,72},{56,64},{64,... | collective-permute-start | bytes 786440 | tf_op jit(solution)/shard_map/ppermute | solution.py:451
  19.1 0.0 collective-permute-start.4
  19.1 0.1 convert_reduce_fusion
  19.2 0.7 select_reduce_fusion.3
  20.0 0.2 select_reduce_fusion
  20.1 0.2 fusion.18
  20.3 0.2 select_reduce_fusion.7
  20.5 0.2 select_reduce_fusion.6
  20.7 8.6 %collective-permute-done.3.refs_1_ = bf16[4,2,128,128]{3,2,1,0:T(8,128)(2,1)S(1)} collective-permute-done((bf16[4,2,128,128]{3,2,1,0:T(8,128)(2,1)S(1)}, bf16[4,2,128,128]{3,2,1,0:T(8,128)(2,1)S(1)}, u32[]{:S(2)}, u32[]{:S(2)}) %collective-permute-start.3) | collective-permute-done | bytes 262176 | tf_op jit(solution)/shard_map/ppermute | solution.py:451
  29.3 0.0 collective-permute-done.6.refs_4_
  29.3 0.5 collective-permute-start.8
  29.9 1.3 %collective-permute-done.7.refs_5_ = bf16[4,2,128,128]{3,2,1,0:T(8,128)(2,1)S(1)} collective-permute-done((bf16[4,2,128,128]{3,2,1,0:T(8,128)(2,1)S(1)}, bf16[4,2,128,128]{3,2,1,0:T(8,128)(2,1)S(1)}, u32[]{:S(2)}, u32[]{:S(2)}) %collective-permute-start.7) | collective-permute-done | bytes 262176 | tf_op jit(solution)/shard_map/ppermute | solution.py:451
  31.1 0.0 collective-permute-start.9
  31.2 0.1 select_reduce_fusion.8
  32.0 0.2 fusion.16
  32.2 0.1 select_reduce_fusion.2
  32.3 0.1 concatenate.3.sc
  32.4 0.0 collective-permute-done.4.refs_2_
  32.4 0.0 collective-permute-done.5.refs_3_
  32.4 0.0 collective-permute-done.8.refs_6_
  32.4 0.4 collective-permute-done.9.refs_7_
  32.8 3.3 %window_keys.1 = (bf16[4096,128]{1,0:T(8,128)(2,1)S(1)}, bf16[4096,128]{1,0:T(8,128)(2,1)S(1)}, bf16[8,128,512]{2,1,0:T(8,128)(2,1)S(1)}, bf16[8,128,512]{2,1,0:T(8,128)(2,1)S(1)}, f32[1,512]{1,0:T(1,128)S(1)}) custom-call(s32[177]{0:T(256)S(1)} %concatenate.3.sc, bf16[4,2,128,128]{3,2,1,0:T(8,128)(2,1)S(1)} %pad_maximum_fusion.1.refs_0_, ...), custom_call_target="tpu_custom_call" | custom-call | flops 1048576 | bytes 6291456 | tf_op jit(solution)/shard_map/window_keys/pallas_call | solution.py:316
  36.1 0.0 copy-start.1
  36.1 1.0 copy-done.1
  37.1 1.0 copy-done.3
  38.0 1.0 copy-done.5
  39.0 1.0 copy-done.7
  40.0 2.1 %all-to-all-done.rows_ref = bf16[8,2,4,128,128]{4,3,2,1,0:T(8,128)(2,1)S(1)} async-done(((bf16[8,2,4,128,128]{4,3,2,1,0:T(8,128)(2,1)}), bf16[8,2,4,128,128]{4,3,2,1,0:T(8,128)(2,1)S(1)}, u32[]{:S(2)}, u32[]{:S(2)}) %all-to-all-start) | async-done | bytes 2097184 | tf_op jit(solution)/shard_map/all_to_all | solution.py:475
  42.1 1.2 copy-done.2
  43.3 1.2 copy-done.4
  44.6 1.2 copy-done.6
  45.8 1.2 copy-done.8
  47.0 27.7 %window_attention.1 = (bf16[8,2,4,128,128]{4,3,2,1,0:T(8,128)(2,1)S(1)}, bf16[2,2,4,2,128,128]{5,4,3,2,1,0:T(8,128)(2,1)S(1)}, bf16[2,2,4,2,128,128]{5,4,3,2,1,0:T(8,128)(2,1)}) custom-call(s32[177]{0:T(256)S(1)} %concatenate.3.sc, f32[1,512]{1,0:T(1,128)S(1)} %get-tuple-element.25.long_ref, bf16[8,2,4,128,128]{4,3,2,1,0:T(8,128)(2,1)S(1)} %all-to-all-done.rows_ref, ...), custom_call_target="tpu_custom_call" | custom-call | flops 21474836480 | bytes 6291456 | tf_op jit(solution)/shard_map/window_attention/pallas_call | solution.py:316
  74.7 1.3 %copy-done = bf16[8,2,4,128,128]{4,3,2,1,0:T(8,128)(2,1)} copy-done((bf16[8,2,4,128,128]{4,3,2,1,0:T(8,128)(2,1)}, bf16[8,2,4,128,128]{4,3,2,1,0:T(8,128)(2,1)S(1)}, u32[]{:S(2)}) %copy-start) | copy-done | bytes 2097176
  76.1 0.0 collective-permute-start.10
  76.1 3.6 %all-to-all-start.1 = ((bf16[8,2,4,128,128]{4,3,2,1,0:T(8,128)(2,1)}), bf16[8,2,4,128,128]{4,3,2,1,0:T(8,128)(2,1)S(1)}, u32[]{:S(2)}, u32[]{:S(2)}) async-start(bf16[8,2,4,128,128]{4,3,2,1,0:T(8,128)(2,1)} %copy-done), calls=%async_computation.1 | async-start | bytes 4194304 | tf_op jit(solution)/shard_map/all_to_all | solution.py:486
  79.7 2.1 %fusion.4 = (bf16[4,2,128,128]{3,2,1,0:T(8,128)(2,1)}, bf16[4,2,128,128]{3,2,1,0:T(8,128)(2,1)S(1)}, bf16[4,2,128,128]{3,2,1,0:T(8,128)(2,1)}) fusion(bf16[2,2,4,2,128,128]{5,4,3,2,1,0:T(8,128)(2,1)} %collective-permute-done.10, bf16[2,2,4,2,128,128]{5,4,3,2,1,0:T(8,128)(2,1)S(1)} %get-tuple-element.32), kind=kLoop, calls=%fused_computation.20 | loop fusion | flops 1572864 | bytes 2359296 | tf_op jit(solution)/shard_map/convert_element_type | solution.py:434
  81.8 14.8 %collective-permute-start.11 = (bf16[4,2,128,128]{3,2,1,0:T(8,128)(2,1)}, bf16[4,2,128,128]{3,2,1,0:T(8,128)(2,1)}, u32[]{:S(2)}, u32[]{:S(2)}) collective-permute-start(bf16[4,2,128,128]{3,2,1,0:T(8,128)(2,1)} %get-tuple-element.61), channel_id=1, source_target_pairs={{0,8},{8,0},{16,24},{24,16},{32,40},{40,32},{48,56},{56,48},{64,72... | collective-permute-start | bytes 786440 | tf_op jit(solution)/shard_map/ppermute | solution.py:451
  96.6 7.5 %collective-permute-done.11 = bf16[4,2,128,128]{3,2,1,0:T(8,128)(2,1)} collective-permute-done((bf16[4,2,128,128]{3,2,1,0:T(8,128)(2,1)}, bf16[4,2,128,128]{3,2,1,0:T(8,128)(2,1)}, u32[]{:S(2)}, u32[]{:S(2)}) %collective-permute-start.11) | collective-permute-done | bytes 262176 | tf_op jit(solution)/shard_map/ppermute | solution.py:451
  104.1 5.5 %collective-permute-done.12 = bf16[4,2,128,128]{3,2,1,0:T(8,128)(2,1)} collective-permute-done((bf16[4,2,128,128]{3,2,1,0:T(8,128)(2,1)}, bf16[4,2,128,128]{3,2,1,0:T(8,128)(2,1)}, u32[]{:S(2)}, u32[]{:S(2)}) %collective-permute-start.12) | collective-permute-done | bytes 262176 | tf_op jit(solution)/shard_map/ppermute | solution.py:451
  109.5 3.8 %collective-permute-done.13 = bf16[4,2,128,128]{3,2,1,0:T(8,128)(2,1)} collective-permute-done((bf16[4,2,128,128]{3,2,1,0:T(8,128)(2,1)S(1)}, bf16[4,2,128,128]{3,2,1,0:T(8,128)(2,1)}, u32[]{:S(2)}, u32[]{:S(2)}) %collective-permute-start.13) | collective-permute-done | bytes 262176 | tf_op jit(solution)/shard_map/ppermute | solution.py:451
  113.3 1.4 %fusion.2 = bf16[4,2,128,128]{3,2,1,0:T(8,128)(2,1)S(1)} fusion(bf16[4,2,128,128]{3,2,1,0:T(8,128)(2,1)} %collective-permute-done.13, bf16[4,2,128,128]{3,2,1,0:T(8,128)(2,1)} %collective-permute-done.12, bf16[4,2,128,128]{3,2,1,0:T(8,128)(2,1)} %collective-permute-done.11, bf16[2,2,4,2,128,128]{5,4,3,2,1,0:T(8,128)(2,1)} %collective-permute-done.10, ...), kind=kLoop, calls=%fused_computation.6 | loop fusion | flops 1572864 | bytes 1572864 | tf_op jit(solution)/shard_map/convert_element_type | solution.py:434
  114.7 2.9 %collective-permute-start.14 = (bf16[2,128,128]{2,1,0:T(8,128)(2,1)S(1)}, bf16[2,128,128]{2,1,0:T(8,128)(2,1)S(1)}, u32[]{:S(2)}, u32[]{:S(2)}) collective-permute-start(bf16[2,128,128]{2,1,0:T(8,128)(2,1)S(1)} %get-tuple-element.74), channel_id=1, source_target_pairs={{0,6},{2,0},{4,2},{6,4},{1,7},{3,1},{5,3},{7,5},{8,14},{10,8},{12,... | collective-permute-start | bytes 196616 | tf_op jit(solution)/shard_map/ppermute | solution.py:438
  117.6 0.8 collective-permute-start.15
  118.5 0.9 collective-permute-start.16
  119.4 0.1 fusion.31
  119.5 1.6 %copy.36 = bf16[32,128,128]{2,0,1:T(8,128)(2,1)} copy(bf16[32,128,128]{2,1,0:T(8,128)(2,1)S(1)} %bitcast.64) | data formatting | bytes 2097152 | tf_op jit(solution)/shard_map/reshape;squeeze | solution.py:489
  121.1 1.6 %copy.37 = bf16[32,128,128]{2,0,1:T(8,128)(2,1)} copy(bf16[32,128,128]{2,1,0:T(8,128)(2,1)S(1)} %bitcast.63) | data formatting | bytes 2097152 | tf_op jit(solution)/shard_map/reshape;squeeze | solution.py:489
  122.8 0.6 collective-permute-done.15
  123.4 0.7 collective-permute-done.16
  124.2 0.8 copy.30
  125.0 0.8 copy.31
  (36 shorter events, 0.3 us)
Async XLA Ops:
  0.6 8.6 %copy-start.9 = (bf16[128,32,128]{2,1,0:T(8,128)(2,1)S(1)}, bf16[128,32,128]{2,1,0:T(8,128)(2,1)}, u32[]{:S(2)}) copy-start(bf16[128,32,128]{2,1,0:T(8,128)(2,1)} %param.9) | copy-start | bytes 3145732
  1.8 9.3 %collective-permute-start = (bf16[2,128,128]{2,1,0:T(8,128)(2,1)S(1)}, bf16[2,128,128]{2,1,0:T(8,128)(2,1)S(1)}, u32[]{:S(2)}, u32[]{:S(2)}) collective-permute-start(bf16[2,128,128]{2,1,0:T(8,128)(2,1)S(1)} %get-tuple-element.77), channel_id=1, source_target_pairs={{0,2},{2,4},{4,6},{6,0},{1,3},{3,5},{5,7},{7,1},{8,10},{10,12},{12... | collective-permute-start | bytes 196616 | tf_op jit(solution)/shard_map/ppermute | solution.py:438
  3.4 7.8 %collective-permute-start.1 = (bf16[2,128,128]{2,1,0:T(8,128)(2,1)S(1)}, bf16[2,128,128]{2,1,0:T(8,128)(2,1)S(1)}, u32[]{:S(2)}, u32[]{:S(2)}) collective-permute-start(bf16[2,128,128]{2,1,0:T(8,128)(2,1)S(1)} %get-tuple-element.78), channel_id=1, source_target_pairs={{0,4},{2,6},{4,0},{6,2},{1,5},{3,7},{5,1},{7,3},{8,12},{10,14},{12... | collective-permute-start | bytes 196616 | tf_op jit(solution)/shard_map/ppermute | solution.py:438
  6.1 5.0 %collective-permute-start.2 = (bf16[2,128,128]{2,1,0:T(8,128)(2,1)S(1)}, bf16[2,128,128]{2,1,0:T(8,128)(2,1)S(1)}, u32[]{:S(2)}, u32[]{:S(2)}) collective-permute-start(bf16[2,128,128]{2,1,0:T(8,128)(2,1)S(1)} %get-tuple-element.79), channel_id=1, source_target_pairs={{0,6},{2,0},{4,2},{6,4},{1,7},{3,1},{5,3},{7,5},{8,14},{10,8},{12,... | collective-permute-start | bytes 196616 | tf_op jit(solution)/shard_map/ppermute | solution.py:438
  11.2 7.9 %copy-start.10 = (s32[256,128]{1,0:T(8,128)S(1)}, s32[256,128]{1,0:T(8,128)}, u32[]{:S(2)}) copy-start(s32[256,128]{1,0:T(8,128)} %param.10) | copy-start | bytes 393220
  11.2 8.0 %copy-start.11 = (s32[256]{0:T(256)S(1)}, s32[256]{0:T(256)}, u32[]{:S(2)}) copy-start(s32[256]{0:T(256)} %param.11) | copy-start | bytes 3076
  11.2 30.9 %all-to-all-start = ((bf16[8,2,4,128,128]{4,3,2,1,0:T(8,128)(2,1)}), bf16[8,2,4,128,128]{4,3,2,1,0:T(8,128)(2,1)S(1)}, u32[]{:S(2)}, u32[]{:S(2)}) async-start(bf16[8,2,4,128,128]{4,3,2,1,0:T(8,128)(2,1)} %pad_maximum_fusion), calls=%async_computation | async-start | bytes 4194304 | tf_op jit(solution)/shard_map/all_to_all | solution.py:475
  15.0 14.3 %collective-permute-start.3 = (bf16[4,2,128,128]{3,2,1,0:T(8,128)(2,1)S(1)}, bf16[4,2,128,128]{3,2,1,0:T(8,128)(2,1)S(1)}, u32[]{:S(2)}, u32[]{:S(2)}) collective-permute-start(bf16[4,2,128,128]{3,2,1,0:T(8,128)(2,1)S(1)} %pad_maximum_fusion.1.refs_0_), channel_id=1, source_target_pairs={{0,8},{8,0},{16,24},{24,16},{32,40},{40,32},{48,56},{56,48},{64,72... | collective-permute-start | bytes 786440 | tf_op jit(solution)/shard_map/ppermute | solution.py:451
  16.4 12.9 %collective-permute-start.6 = (bf16[4,2,128,128]{3,2,1,0:T(8,128)(2,1)S(1)}, bf16[4,2,128,128]{3,2,1,0:T(8,128)(2,1)S(1)}, u32[]{:S(2)}, u32[]{:S(2)}) collective-permute-start(bf16[4,2,128,128]{3,2,1,0:T(8,128)(2,1)S(1)} %pad_maximum_fusion.1.refs_0_), channel_id=1, source_target_pairs={{0,16},{8,24},{16,32},{24,40},{32,48},{40,56},{48,64},{56,72},{64,... | collective-permute-start | bytes 786440 | tf_op jit(solution)/shard_map/ppermute | solution.py:451
  17.5 13.6 %collective-permute-start.7 = (bf16[4,2,128,128]{3,2,1,0:T(8,128)(2,1)S(1)}, bf16[4,2,128,128]{3,2,1,0:T(8,128)(2,1)S(1)}, u32[]{:S(2)}, u32[]{:S(2)}) collective-permute-start(bf16[4,2,128,128]{3,2,1,0:T(8,128)(2,1)S(1)} %pad_maximum_fusion.1.refs_0_), channel_id=1, source_target_pairs={{0,24},{8,16},{16,40},{24,32},{32,56},{40,48},{48,72},{56,64},{64,... | collective-permute-start | bytes 786440 | tf_op jit(solution)/shard_map/ppermute | solution.py:451
  19.1 13.3 %collective-permute-start.4 = (bf16[4,2,128,128]{3,2,1,0:T(8,128)(2,1)S(1)}, bf16[4,2,128,128]{3,2,1,0:T(8,128)(2,1)S(1)}, u32[]{:S(2)}, u32[]{:S(2)}) collective-permute-start(bf16[4,2,128,128]{3,2,1,0:T(8,128)(2,1)S(1)} %pad_maximum_fusion.1.refs_0_), channel_id=1, source_target_pairs={{0,1},{1,0},{2,3},{3,2},{4,5},{5,4},{6,7},{7,6},{8,9},{9,8},{10,11... | collective-permute-start | bytes 786440 | tf_op jit(solution)/shard_map/ppermute | solution.py:442
  29.3 3.1 %collective-permute-start.5 = (bf16[4,2,128,128]{3,2,1,0:T(8,128)(2,1)S(1)}, bf16[4,2,128,128]{3,2,1,0:T(8,128)(2,1)}, u32[]{:S(2)}, u32[]{:S(2)}) collective-permute-start(bf16[4,2,128,128]{3,2,1,0:T(8,128)(2,1)S(1)} %collective-permute-done.3.refs_1_), channel_id=1, source_target_pairs={{0,1},{1,0},{2,3},{3,2},{4,5},{5,4},{6,7},{7,6},{8,9},{9,8},{10,11... | collective-permute-start | bytes 786440 | tf_op jit(solution)/shard_map/ppermute | solution.py:442
  29.3 3.1 %collective-permute-start.8 = (bf16[4,2,128,128]{3,2,1,0:T(8,128)(2,1)S(1)}, bf16[4,2,128,128]{3,2,1,0:T(8,128)(2,1)}, u32[]{:S(2)}, u32[]{:S(2)}) collective-permute-start(bf16[4,2,128,128]{3,2,1,0:T(8,128)(2,1)S(1)} %collective-permute-done.6.refs_4_), channel_id=1, source_target_pairs={{0,1},{1,0},{2,3},{3,2},{4,5},{5,4},{6,7},{7,6},{8,9},{9,8},{10,11... | collective-permute-start | bytes 786440 | tf_op jit(solution)/shard_map/ppermute | solution.py:442
  31.1 1.7 %collective-permute-start.9 = (bf16[4,2,128,128]{3,2,1,0:T(8,128)(2,1)S(1)}, bf16[4,2,128,128]{3,2,1,0:T(8,128)(2,1)}, u32[]{:S(2)}, u32[]{:S(2)}) collective-permute-start(bf16[4,2,128,128]{3,2,1,0:T(8,128)(2,1)S(1)} %collective-permute-done.7.refs_5_), channel_id=1, source_target_pairs={{0,1},{1,0},{2,3},{3,2},{4,5},{5,4},{6,7},{7,6},{8,9},{9,8},{10,11... | collective-permute-start | bytes 786440 | tf_op jit(solution)/shard_map/ppermute | solution.py:442
  36.1 1.0 copy-start.1
  37.1 1.0 copy-start.3
  38.0 1.0 copy-start.5
  39.0 1.0 copy-start.7
  42.1 1.2 copy-start.2
  43.3 1.2 copy-start.4
  44.5 1.2 copy-start.6
  45.8 1.2 copy-start.8
  74.7 1.3 %copy-start = (bf16[8,2,4,128,128]{4,3,2,1,0:T(8,128)(2,1)}, bf16[8,2,4,128,128]{4,3,2,1,0:T(8,128)(2,1)S(1)}, u32[]{:S(2)}) copy-start(bf16[8,2,4,128,128]{4,3,2,1,0:T(8,128)(2,1)S(1)} %get-tuple-element.31) | copy-start | bytes 6291460
  76.1 3.6 %collective-permute-start.10 = (bf16[2,2,4,2,128,128]{5,4,3,2,1,0:T(8,128)(2,1)}, bf16[2,2,4,2,128,128]{5,4,3,2,1,0:T(8,128)(2,1)}, u32[]{:S(2)}, u32[]{:S(2)}) collective-permute-start(bf16[2,2,4,2,128,128]{5,4,3,2,1,0:T(8,128)(2,1)} %get-tuple-element.33), channel_id=1, source_target_pairs={{0,1},{1,0},{2,3},{3,2},{4,5},{5,4},{6,7},{7,6},{8,9},{9,8},{10,11... | collective-permute-start | bytes 3145736 | tf_op jit(solution)/shard_map/ppermute | solution.py:442
  76.1 43.3 %all-to-all-start.1 = ((bf16[8,2,4,128,128]{4,3,2,1,0:T(8,128)(2,1)}), bf16[8,2,4,128,128]{4,3,2,1,0:T(8,128)(2,1)S(1)}, u32[]{:S(2)}, u32[]{:S(2)}) async-start(bf16[8,2,4,128,128]{4,3,2,1,0:T(8,128)(2,1)} %copy-done), calls=%async_computation.1 | async-start | bytes 4194304 | tf_op jit(solution)/shard_map/all_to_all | solution.py:486
  81.8 22.2 %collective-permute-start.11 = (bf16[4,2,128,128]{3,2,1,0:T(8,128)(2,1)}, bf16[4,2,128,128]{3,2,1,0:T(8,128)(2,1)}, u32[]{:S(2)}, u32[]{:S(2)}) collective-permute-start(bf16[4,2,128,128]{3,2,1,0:T(8,128)(2,1)} %get-tuple-element.61), channel_id=1, source_target_pairs={{0,8},{8,0},{16,24},{24,16},{32,40},{40,32},{48,56},{56,48},{64,72... | collective-permute-start | bytes 786440 | tf_op jit(solution)/shard_map/ppermute | solution.py:451
  96.6 12.9 %collective-permute-start.12 = (bf16[4,2,128,128]{3,2,1,0:T(8,128)(2,1)}, bf16[4,2,128,128]{3,2,1,0:T(8,128)(2,1)}, u32[]{:S(2)}, u32[]{:S(2)}) collective-permute-start(bf16[4,2,128,128]{3,2,1,0:T(8,128)(2,1)} %get-tuple-element.63), channel_id=1, source_target_pairs={{0,240},{8,248},{16,0},{24,8},{32,16},{40,24},{48,32},{56,40},{64,... | collective-permute-start | bytes 786440 | tf_op jit(solution)/shard_map/ppermute | solution.py:451
  96.6 16.7 %collective-permute-start.13 = (bf16[4,2,128,128]{3,2,1,0:T(8,128)(2,1)S(1)}, bf16[4,2,128,128]{3,2,1,0:T(8,128)(2,1)}, u32[]{:S(2)}, u32[]{:S(2)}) collective-permute-start(bf16[4,2,128,128]{3,2,1,0:T(8,128)(2,1)S(1)} %get-tuple-element.62), channel_id=1, source_target_pairs={{0,248},{8,240},{16,8},{24,0},{32,24},{40,16},{48,40},{56,32},{64,... | collective-permute-start | bytes 786440 | tf_op jit(solution)/shard_map/ppermute | solution.py:451
  114.7 8.1 %collective-permute-start.14 = (bf16[2,128,128]{2,1,0:T(8,128)(2,1)S(1)}, bf16[2,128,128]{2,1,0:T(8,128)(2,1)S(1)}, u32[]{:S(2)}, u32[]{:S(2)}) collective-permute-start(bf16[2,128,128]{2,1,0:T(8,128)(2,1)S(1)} %get-tuple-element.74), channel_id=1, source_target_pairs={{0,6},{2,0},{4,2},{6,4},{1,7},{3,1},{5,3},{7,5},{8,14},{10,8},{12,... | collective-permute-start | bytes 196616 | tf_op jit(solution)/shard_map/ppermute | solution.py:438
  117.6 5.8 %collective-permute-start.15 = (bf16[2,128,128]{2,1,0:T(8,128)(2,1)S(1)}, bf16[2,128,128]{2,1,0:T(8,128)(2,1)S(1)}, u32[]{:S(2)}, u32[]{:S(2)}) collective-permute-start(bf16[2,128,128]{2,1,0:T(8,128)(2,1)S(1)} %get-tuple-element.73), channel_id=1, source_target_pairs={{0,4},{2,6},{4,0},{6,2},{1,5},{3,7},{5,1},{7,3},{8,12},{10,14},{12... | collective-permute-start | bytes 196616 | tf_op jit(solution)/shard_map/ppermute | solution.py:438
  118.5 5.6 %collective-permute-start.16 = (bf16[2,128,128]{2,1,0:T(8,128)(2,1)S(1)}, bf16[2,128,128]{2,1,0:T(8,128)(2,1)S(1)}, u32[]{:S(2)}, u32[]{:S(2)}) collective-permute-start(bf16[2,128,128]{2,1,0:T(8,128)(2,1)S(1)} %get-tuple-element.72), channel_id=1, source_target_pairs={{0,2},{2,4},{4,6},{6,0},{1,3},{3,5},{5,7},{7,1},{8,10},{10,12},{12... | collective-permute-start | bytes 196616 | tf_op jit(solution)/shard_map/ppermute | solution.py:438
